TPU v7x, 256 devices: a whole 4x4x8 slice. The times are simulated.
256 devices in a mesh: ctx: 32 (over y, z), tp: 8 (over x, core).
Axes of the slice: x: 4, y: 4, z: 8, core: 2. Of those that a mesh axis runs over, the one named last changes fastest.
Arguments:
- context_block_rows: bfloat16 [16384, 8192], P('ctx', 'tp'), may hold values from -16 to 16
- query_hidden_rows: bfloat16 [64, 8192], P(None, 'tp'), may hold values from -16 to 16
- query_token_positions: int32 [64], replicated, may hold values from 16384 to 16573, as said below
- query_bound: int32 [64], replicated, may hold values from 1 to 16384, as said below
- query_matrix: bfloat16 [8192, 8192], P('ctx', 'tp'), may hold values from -0.0625 to 0.0625
- key_matrix: bfloat16 [8192, 1024], P('ctx', 'tp'), may hold values from -0.0625 to 0.0625
- value_matrix: bfloat16 [8192, 1024], P('ctx', 'tp'), may hold values from -0.0625 to 0.0625
Outputs:
- block_out: bfloat16 [16384, 8192], P('ctx', 'tp')
- query_out: bfloat16 [64, 8192], P(None, 'tp')
Inputs may be any that keep to these rules, and one draw needn't show every extreme that they name: query_token_positions rise strictly with the index; the first is 16384 and the last 16573. `query_bound`: some query token sees all 16384 context tokens.
All inputs are finite; a program needn't handle non-finite values.
Results may differ from a plain program's by a relative error of at most 0.0059.
The roundings to bfloat16 on the way count: a program that leaves them out, or rounds other values in their place, can miss the bound.
Values may be sent and summed in bfloat16 or wider, within the bound.
A program may use at most 128 MiB of HBM per device.

v0:
```python
import math
import jax
import jax.numpy as jnp
from jax import lax
from jax.sharding import PartitionSpec as P

HEAD_SIZE = 128


def from_root(value, axis, source):
    kept = jnp.where(lax.axis_index(axis) == source, value, 0).astype(value.dtype)
    return lax.psum(kept, axis)


def rope_table(half):
    values = []
    for index in range(half):
        freq = 500000.0 ** (-2.0 * index / (2.0 * half))
        wavelen = 2.0 * math.pi / freq
        if wavelen > 8192.0:
            values.append(freq / 8.0)
        elif wavelen < 2048.0:
            values.append(freq)
        else:
            smooth = (8192.0 / wavelen - 1.0) / 3.0
            values.append((1.0 - smooth) * freq / 8.0 + smooth * freq)
    return values


def apply_rotary(values, token_positions):
    half = values.shape[-1] // 2
    freqs = jnp.asarray(rope_table(half), jnp.float32)
    angle = token_positions.astype(jnp.float32)[:, None] * freqs[None, :]
    cosine = jnp.cos(angle)[:, None, :]
    sine = jnp.sin(angle)[:, None, :]
    first = values[..., :half]
    second = values[..., half:]
    return jnp.concatenate([first * cosine - second * sine, second * cosine + first * sine], -1)


def attend(query_heads_split, keys, values, valid):
    scale = 1.0 / math.sqrt(query_heads_split.shape[-1])
    scores = (
        jnp.einsum("qkgd,skd->qkgs", query_heads_split, keys, preferred_element_type=jnp.float32)
        * scale
    )
    scores = jnp.where(valid[:, None, None, :], scores, -1e30)
    peak = jnp.max(scores, -1)
    weights = jnp.exp(scores - peak[..., None])
    total = jnp.sum(weights, -1)
    mixed = jnp.einsum(
        "qkgs,skd->qkgd", weights.astype(jnp.bfloat16), values, preferred_element_type=jnp.float32
    )
    return (peak, total, mixed)


def on_device(
    context_block_rows,
    query_hidden_rows,
    query_token_positions,
    query_bound,
    query_matrix,
    key_matrix,
    value_matrix,
):
    ctx_index = lax.axis_index("ctx")
    blk = context_block_rows.shape[0]
    qcount = query_hidden_rows.shape[0]
    heads_q = query_matrix.shape[1] // HEAD_SIZE
    heads_kv = key_matrix.shape[1] // HEAD_SIZE
    head_group = heads_q // heads_kv
    whole_rows, whole_query = (
        lax.all_gather(context_block_rows, "tp", axis=1, tiled=True),
        lax.all_gather(query_hidden_rows, "tp", axis=1, tiled=True),
    )
    stacked = jnp.concatenate([whole_rows, whole_query], 0)
    head_rows = blk + qcount
    proj_query = jnp.dot(
        stacked,
        lax.all_gather(query_matrix, "ctx", axis=0, tiled=True),
        preferred_element_type=jnp.float32,
    )
    proj_key = jnp.dot(
        stacked,
        lax.all_gather(key_matrix, "ctx", axis=0, tiled=True),
        preferred_element_type=jnp.float32,
    )
    proj_value = jnp.dot(
        stacked,
        lax.all_gather(value_matrix, "ctx", axis=0, tiled=True),
        preferred_element_type=jnp.float32,
    )
    local_pos = ctx_index * blk + jnp.arange(blk, dtype=jnp.int32)
    k_block = apply_rotary(proj_key[:blk].reshape(blk, heads_kv, HEAD_SIZE), local_pos).astype(
        jnp.bfloat16
    )
    v_block = proj_value[:blk].reshape(blk, heads_kv, HEAD_SIZE).astype(jnp.bfloat16)
    key_token_rows = apply_rotary(
        proj_key[blk:head_rows].reshape(qcount, heads_kv, HEAD_SIZE), query_token_positions
    ).astype(jnp.bfloat16)
    value_token_rows = (
        proj_value[blk:head_rows].reshape(qcount, heads_kv, HEAD_SIZE).astype(jnp.bfloat16)
    )
    anchor_key, anchor_value = (from_root(k_block, "ctx", 0), from_root(v_block, "ctx", 0))
    q_block = apply_rotary(proj_query[:blk].reshape(blk, heads_q, HEAD_SIZE), local_pos).astype(
        jnp.bfloat16
    )
    query_token_rows = (
        apply_rotary(proj_query[blk:].reshape(qcount, heads_q, HEAD_SIZE), query_token_positions)
        .astype(jnp.bfloat16)
        .reshape(qcount, heads_kv, head_group, HEAD_SIZE)
    )
    keys_cat = jnp.concatenate([anchor_key, k_block], 0)
    values_cat = jnp.concatenate([anchor_value, v_block], 0)
    anchor_live = ctx_index > 0
    rows_step = min(blk, 512)
    rows_here = 0 + jnp.arange(rows_step, dtype=jnp.int32)
    valid = jnp.concatenate(
        [
            jnp.broadcast_to(anchor_live, (rows_step, blk)),
            rows_here[:, None] >= jnp.arange(blk, dtype=jnp.int32)[None, :],
        ],
        1,
    )
    query_heads_split = q_block.reshape(rows_step, heads_kv, head_group, HEAD_SIZE)
    peak, total, mixed = attend(query_heads_split, keys_cat, values_cat, valid)
    outputs = (
        (mixed / total[..., None]).astype(jnp.bfloat16).reshape(rows_step, heads_q * HEAD_SIZE)
    )
    valid_ctx = local_pos[None, :] < query_bound[:, None]
    peak, total, mixed = attend(query_token_rows, k_block, v_block, valid_ctx)
    top = lax.pmax(peak, "ctx")
    scaled = jnp.exp(peak - top)
    total_all, mixed_all = lax.psum((total * scaled, mixed * scaled[..., None]), "ctx")
    own = jnp.arange(qcount, dtype=jnp.int32)
    self_peak, self_total, self_mixed = attend(
        query_token_rows, key_token_rows, value_token_rows, own[:, None] >= own[None, :]
    )
    final = jnp.maximum(top, self_peak)
    w_ctx = jnp.exp(top - final)
    w_self = jnp.exp(self_peak - final)
    query_out = (mixed_all * w_ctx[..., None] + self_mixed * w_self[..., None]) / (
        total_all * w_ctx + self_total * w_self
    )[..., None]
    query_out = query_out.astype(jnp.bfloat16).reshape(qcount, heads_q * HEAD_SIZE)
    return (outputs, query_out)


def solution(mesh):
    placed = (
        P("ctx", "tp"),
        P(None, "tp"),
        P(),
        P(),
        P("ctx", "tp"),
        P("ctx", "tp"),
        P("ctx", "tp"),
    )
    return jax.shard_map(
        on_device,
        mesh=mesh,
        in_specs=placed,
        out_specs=(P("ctx", "tp"), P(None, "tp")),
        check_vma=False,
    )
```

profile of v0, /device:TPU:2, one launch (start us, length us, event | category | flops | bytes accessed | tf_op | source)
XLA Modules:
  0.0 689.7 jit_solution(3943614140132584248)
XLA Ops:
  7.2 0.0 all-gather.6.cloned.1.call-start
  7.2 0.7 all-gather.6.cloned.1.call-update
  7.9 0.0 all-gather.8.cloned.1.call-start
  7.9 0.7 all-gather.8.cloned.1.call-update
  8.6 0.0 all-gather.12.cloned.1.call-start
  8.7 0.7 all-gather.12.cloned.1.call-update
  9.4 0.0 all-gather.10.cloned.1.call-start
  9.4 0.5 all-gather.10.cloned.1.call-update
  10.0 0.0 all-gather.14.cloned.1.call-start
  10.0 0.5 all-gather.14.cloned.1.call-update
  10.5 0.0 all-reduce.7.cloned.1.call-start
  10.6 0.7 convert_element_type.69
  11.3 0.1 iota_compare_fusion
  11.3 0.9 concatenate.62
  12.3 1.4 broadcast_compare_fusion
  13.6 0.8 multiply_cosine_fusion.3
  14.5 2.5 multiply_cosine_fusion
  17.0 47.3 %all-gather.6.cloned.1.call-done = bf16[512,8192]{1,0:T(8,128)(2,1)} async-done(((bf16[512,1024]{1,0:T(8,128)(2,1)}), bf16[512,8192]{1,0:T(8,128)(2,1)}) %all-gather.6.cloned.1.call-update) | async-done | bytes 8388624 | tf_op jit(solution)/shard_map/all_gather | solution.py:73
  64.3 7.6 %constant_dynamic-update-slice_fusion.1 = bf16[576,8192]{1,0:T(8,128)(2,1)} fusion(bf16[512,8192]{1,0:T(8,128)(2,1)} %all-gather.6.cloned.1.call-done), kind=kLoop, calls=%fused_computation.100 | loop fusion | bytes 16777216
  71.9 19.5 %all-gather.8.cloned.1.call-done = bf16[64,8192]{1,0:T(8,128)(2,1)} async-done(((bf16[64,1024]{1,0:T(8,128)(2,1)}), bf16[64,8192]{1,0:T(8,128)(2,1)}) %all-gather.8.cloned.1.call-update) | async-done | bytes 1048592 | tf_op jit(solution)/shard_map/all_gather | solution.py:74
  91.4 2.3 constant_dynamic-update-slice_fusion
  93.7 79.8 %all-gather.12.cloned.1.call-done = bf16[8192,128]{1,0:T(8,128)(2,1)} async-done(((bf16[256,128]{1,0:T(8,128)(2,1)}), bf16[8192,128]{1,0:T(8,128)(2,1)}) %all-gather.12.cloned.1.call-update) | async-done | bytes 2097168 | tf_op jit(solution)/shard_map/all_gather | solution.py:85
  173.5 5.8 fusion.83
  179.4 0.0 copy-done.9
  179.4 1.2 fusion.35
  180.6 0.0 copy-start.1
  180.6 0.8 maximum_select_fusion
  181.4 0.8 fusion.64
  182.2 68.9 %all-gather.10.cloned.1.call-done = bf16[8192,128]{1,0:T(8,128)(2,1)} async-done(((bf16[256,128]{1,0:T(8,128)(2,1)}), bf16[8192,128]{1,0:T(8,128)(2,1)}) %all-gather.10.cloned.1.call-update) | async-done | bytes 2097168 | tf_op jit(solution)/shard_map/all_gather | solution.py:90
  251.1 6.9 convolution_convert_fusion
  258.0 0.0 copy-start.2
  258.0 0.7 slice_bitcast_fusion.3
  258.8 0.0 all-reduce.7.cloned.1.call-update
  258.8 0.0 all-reduce.5.cloned.1.call-start
  258.9 132.5 %all-gather.14.cloned.1.call-done = bf16[8192,1024]{1,0:T(8,128)(2,1)} async-done(((bf16[256,1024]{1,0:T(8,128)(2,1)}), bf16[8192,1024]{1,0:T(8,128)(2,1)}) %all-gather.14.cloned.1.call-update) | async-done | bytes 16777232 | tf_op jit(solution)/shard_map/all_gather | solution.py:80
  391.4 0.0 copy-done.2
  391.4 14.9 %fusion.84 = f32[576,1024]{1,0:T(8,128)S(1)} fusion(bf16[576,8192]{1,0:T(8,128)(2,1)} %constant_dynamic-update-slice_fusion, bf16[8192,1024]{1,0:T(8,128)(2,1)} %all-gather.14.cloned.1.call-done), kind=kOutput, calls=%fused_computation.126 | convolution fusion | flops 9663676416 | bytes 28573696 | tf_op jit(solution)/shard_map/dot_general | solution.py:78
  406.4 0.1 slice_bitcast_fusion
  406.6 0.1 fusion.80
  406.7 0.1 subtract_convert_fusion.1
  406.8 1.4 fusion.81
  408.2 1.0 fusion.25
  409.1 71.4 %pmax.7 = f32[64,1,8]{0,2,1:T(8,128)S(1)} all-reduce(f32[64,1,8]{0,2,1:T(8,128)S(1)} %bitcast.169), channel_id=1, replica_groups=mesh['ctx'=32,'tp'=8] {'ctx'}, use_global_device_ids=true, to_apply=%region_5.6 | all-reduce | flops 512 | bytes 4096 | tf_op jit(solution)/shard_map/pmax | solution.py:132
  480.6 0.0 copy-start.7
  480.6 0.5 copy.38
  481.1 2.0 fusion.79
  483.1 0.0 copy-done.7
  483.1 0.6 bitcast_multiply_fusion.1
  483.7 1.1 fusion.14
  484.7 0.0 all-reduce.5.cloned.1.call-update
  484.8 3.5 subtract_convert_fusion
  488.2 47.8 %all-reduce.7.cloned.1.call-done = (bf16[512,1,128]{2,0,1:T(8,128)(2,1)}, bf16[512,1,128]{2,0,1:T(8,128)(2,1)}) async-done(((bf16[512,1,128]{2,0,1:T(8,128)(2,1)}, bf16[512,1,128]{2,0,1:T(8,128)(2,1)}), (bf16[512,1,128]{2,0,1:T(8,128)(2,1)}, bf16[512,1,128]{2,0,1:T(8,128)(2,1)})) %all-reduce.7.cloned.1.call-update) | async-done | bytes 262160 | tf_op jit(solution)/shard_map/psum | solution.py:12
  536.1 10.7 %fusion.2 = (f32[512,8]{0,1:T(8,128)S(1)}, f32[1024,512,8]{1,0,2:T(8,128)}) fusion(pred[512,1024]{0,1:T(8,128)(4,1)} %concatenate.62, bf16[512,8,64]{2,0,1:T(8,128)(2,1)} %get-tuple-element.9, bf16[512,8,64]{2,0,1:T(8,128)(2,1)S(1)} %get-tuple-element.8, bf16[512,1,64]{2,0,1:T(8,128)(2,1)} %copy-done.1, bf16[512,1,64]{2,0,1:T(8,128)(2,1)S(1)} %get-tuple-element.14, ...), kind=kOutput, calls=%fused_computation.4 | convolution fusion | flops 1089204224 | bytes 18628608 | tf_op jit(solution)/shard_map/qkgd,skd->qkgs/dot_general | solution.py:44
  546.8 0.0 copy-done
  546.8 9.3 %fusion = f32[512,8]{0,1:T(8,128)S(1)} fusion(f32[1024,512,8]{1,0,2:T(8,128)} %get-tuple-element.32, f32[512,8]{0,1:T(8,128)S(1)} %get-tuple-element.31, pred[512,1024]{0,1:T(8,128)(4,1)S(1)} %copy-done), kind=kLoop, calls=%fused_computation.2 | loop fusion | flops 16773120 | bytes 17334272 | tf_op jit(solution)/shard_map/reduce_sum | solution.py:50
  556.1 0.3 fusion.82
  556.5 9.1 %fusion.7 = bf16[1,128,512,8]{2,1,3,0:T(8,128)(2,1)S(1)} fusion(f32[1024,512,8]{1,0,2:T(8,128)} %get-tuple-element.32, f32[512,8]{0,1:T(8,128)S(1)} %get-tuple-element.31, pred[512,1024]{0,1:T(8,128)(4,1)S(1)} %copy-done, f32[512,8]{0,1:T(8,128)S(1)} %fusion, bf16[512,1,128]{2,0,1:T(8,128)(2,1)S(1)} %copy-done.4, bf16[512,1,128]{2,0,1:T(8,128)(2,1)S(1)} %copy-done.10), kind=kOutput, calls=%fused_computation.10 | convolution fusion | flops 1092091904 | bytes 18644992 | tf_op jit(solution)/shard_map/qkgs,skd->qkgd/dot_general | solution.py:51
  565.6 0.1 fusion.44
  565.7 1.3 copy.29
  567.0 72.5 %psum.31 = f32[64,1,8]{0,2,1:T(8,128)S(1)} all-reduce(f32[64,1,8]{0,2,1:T(8,128)S(1)} %copy-done.8), channel_id=1, replica_groups=mesh['ctx'=32,'tp'=8] {'ctx'}, use_global_device_ids=true, to_apply=%region_9.10 | all-reduce | flops 512 | bytes 4096 | tf_op jit(solution)/shard_map/psum | solution.py:134
  639.5 41.2 %all-reduce.5.cloned.1.call-done = f32[64,1,8,128]{3,0,2,1:T(8,128)} async-done(((f32[64,1,8,128]{3,0,2,1:T(8,128)}), f32[64,1,8,128]{3,0,2,1:T(8,128)}) %all-reduce.5.cloned.1.call-update) | async-done | bytes 262160 | tf_op jit(solution)/shard_map/psum | solution.py:134
  680.7 1.3 fusion.19
  682.0 0.1 copy.28
  682.1 0.7 copy.50
  (23 shorter events, 0.1 us)
Async XLA Ops:
  7.2 57.1 %all-gather.6.cloned.1.call-start = ((), (), s32[]{:S(2)}) async-start(), calls=%async_computation | async-start | bytes 9437184 | tf_op jit(solution)/shard_map/all_gather | solution.py:73
  7.9 83.5 %all-gather.8.cloned.1.call-start = ((), (), s32[]{:S(2)}) async-start(), calls=%async_computation.1 | async-start | bytes 1179648 | tf_op jit(solution)/shard_map/all_gather | solution.py:74
  8.6 164.9 %all-gather.12.cloned.1.call-start = ((), (), s32[]{:S(2)}) async-start(), calls=%async_computation.3 | async-start | bytes 2162688 | tf_op jit(solution)/shard_map/all_gather | solution.py:85
  9.4 241.7 %all-gather.10.cloned.1.call-start = ((), (), s32[]{:S(2)}) async-start(), calls=%async_computation.2 | async-start | bytes 2162688 | tf_op jit(solution)/shard_map/all_gather | solution.py:90
  10.0 381.4 %all-gather.14.cloned.1.call-start = ((), (), s32[]{:S(2)}) async-start(), calls=%async_computation.4 | async-start | bytes 17301504 | tf_op jit(solution)/shard_map/all_gather | solution.py:80
  10.5 525.5 %all-reduce.7.cloned.1.call-start = ((), (), s32[]{:S(2)}) async-start(), calls=%async_computation.6 | async-start | bytes 524288 | tf_op jit(solution)/shard_map/psum | solution.py:12
  71.9 107.5 %copy-start.9 = (f32[64]{0:T(128)S(1)}, f32[64]{0:T(128)}, u32[]{:S(2)}) copy-start(f32[64]{0:T(128)} %constant.24.clone) | copy-start | bytes 772
  180.6 225.7 %copy-start.1 = (bf16[512,1,64]{2,0,1:T(8,128)(2,1)}, bf16[512,1,64]{2,0,1:T(8,128)(2,1)S(1)}, u32[]{:S(2)}) copy-start(bf16[512,1,64]{2,0,1:T(8,128)(2,1)S(1)} %get-tuple-element.15) | copy-start | bytes 196612
  258.0 133.4 %copy-start.2 = (bf16[576,128]{1,0:T(8,128)(2,1)}, bf16[576,128]{1,0:T(8,128)(2,1)S(1)}, u32[]{:S(2)}) copy-start(bf16[576,128]{1,0:T(8,128)(2,1)S(1)} %convolution_convert_fusion) | copy-start | bytes 442372
  258.8 421.9 %all-reduce.5.cloned.1.call-start = ((), (), s32[]{:S(2)}) async-start(), calls=%async_computation.5 | async-start | bytes 524288 | tf_op jit(solution)/shard_map/psum | solution.py:134
  480.6 2.5 copy-start.7
  480.6 3.1 copy-start.3
  536.1 10.7 %copy-start = (pred[512,1024]{0,1:T(8,128)(4,1)S(1)}, pred[512,1024]{0,1:T(8,128)(4,1)}, u32[]{:S(2)}) copy-start(pred[512,1024]{0,1:T(8,128)(4,1)} %concatenate.62) | copy-start | bytes 1572868
  546.8 9.3 %copy-start.5 = (bf16[64,64]{1,0:T(8,128)(2,1)S(1)}, bf16[64,64]{1,0:T(8,128)(2,1)}, u32[]{:S(2)}) copy-start(bf16[64,64]{1,0:T(8,128)(2,1)} %get-tuple-element.20) | copy-start | bytes 24580
  546.8 9.3 %copy-start.6 = (bf16[64,64]{1,0:T(8,128)(2,1)S(1)}, bf16[64,64]{1,0:T(8,128)(2,1)}, u32[]{:S(2)}) copy-start(bf16[64,64]{1,0:T(8,128)(2,1)} %get-tuple-element.21) | copy-start | bytes 24580
  546.8 9.6 %copy-start.4 = (bf16[512,1,128]{2,0,1:T(8,128)(2,1)S(1)}, bf16[512,1,128]{2,0,1:T(8,128)(2,1)}, u32[]{:S(2)}) copy-start(bf16[512,1,128]{2,0,1:T(8,128)(2,1)} %get-tuple-element.18) | copy-start | bytes 393220
  546.8 9.6 %copy-start.10 = (bf16[512,1,128]{2,0,1:T(8,128)(2,1)S(1)}, bf16[512,1,128]{2,0,1:T(8,128)(2,1)}, u32[]{:S(2)}) copy-start(bf16[512,1,128]{2,0,1:T(8,128)(2,1)} %get-tuple-element.7) | copy-start | bytes 393220
  556.5 10.5 %copy-start.8 = (f32[64,1,8]{0,2,1:T(8,128)S(1)}, f32[64,1,8]{0,2,1:T(8,128)}, u32[]{:S(2)}) copy-start(f32[64,1,8]{0,2,1:T(8,128)} %get-tuple-element.25) | copy-start | bytes 6148
Sparse Core Ops, SparseCore 0:
  9.8 54.4 all-gather.5
  66.1 25.2 all-gather.7
  94.0 79.4 all-gather.11
  176.0 75.1 all-gather.9
  253.6 137.7 all-gather.13
  394.7 141.2 all-reduce.6
  539.5 141.1 all-reduce.4
where the time goes:
time: 690 us
  waiting for transfers between devices  440 us (64%)
  blocking collectives  144 us (21%)
  matrix products  51.5 us (7%)
  other arithmetic  23.5 us (3%)
  local copies, waits for them, and re-layouts  15.8 us (2%)
  between operations  14.4 us (2%)
    all_gather x1, waiting for transfers between devices, on_device(): lax.all_gather(query_matrix, 'ctx', axis=0, tiled=True)  133 us
    all_gather x1, waiting for transfers between devices, on_device(): lax.all_gather(key_matrix, 'ctx', axis=0, tiled=True)  79.8 us
    psum x1, blocking collectives, on_device(): lax.psum((total * scaled, mixed * scaled[..., None]), 'ctx')  72.5 us
    pmax x1, blocking collectives, on_device(): top = lax.pmax(peak, 'ctx')  71.4 us
    all_gather x1, waiting for transfers between devices, on_device(): lax.all_gather(value_matrix, 'ctx', axis=0, tiled=True)  68.9 us
    psum x1, waiting for transfers between devices, from_root(): return lax.psum(kept, axis)  47.8 us
    all_gather x1, waiting for transfers between devices, on_device(): lax.all_gather(context_block_rows, 'tp', axis=1, tiled=True)  47.3 us
    psum x1, waiting for transfers between devices, on_device(): lax.psum((total * scaled, mixed * scaled[..., None]), 'ctx')  41.2 us
  transfers between devices with their start and end apart: 7, of which 7 were waited for; matrix products, arithmetic and copies ran while one was open for 13% of the time, Pallas kernels for 0%

commit v1 on v0

--- a/solution.py
+++ b/solution.py
@@ -1,3 +1,4 @@
+import functools
 import math
 import jax
 import jax.numpy as jnp
@@ -5,6 +6,41 @@
 from jax.sharding import PartitionSpec as P
 
 HEAD_SIZE = 128
+
+
+def settle_outputs(s0, dim_at):
+    s0 = jnp.moveaxis(s0, 0, dim_at)
+    block_now = s0.shape
+    piece_out = s0.reshape(
+        *block_now[:dim_at], block_now[dim_at] * block_now[dim_at + 1], *block_now[dim_at + 2 :]
+    )
+    return piece_out
+
+
+def measure_the_weights(array_in, chip_axis, k_dim):
+    panels = []
+    extent = lax.axis_size(chip_axis)
+    for pp in range(extent):
+        panels.append((pp, (pp + 1) % extent))
+    row_list = []
+    for b, no in panels:
+        row_list.append((no, b))
+    a_now, now = ([], [])
+    for p in range(extent - 1):
+        if p % 2 == 0:
+            opened = lax.ppermute(a_now[-1] if a_now else array_in, chip_axis, panels)
+            a_now.append(opened)
+        else:
+            now.append(lax.ppermute(now[-1] if now else array_in, chip_axis, row_list))
+    carry = jnp.stack([*a_now[::-1], array_in, *now])
+    built = lax.axis_index(chip_axis)
+    high = built - len(a_now)
+    carry = carry[(jnp.arange(extent) - high) % extent]
+    tile_out = settle_outputs(carry, k_dim)
+    return tile_out
+
+
+_save_loads = functools.partial(measure_the_weights, chip_axis="tp", k_dim=1)
 
 
 def from_root(value, axis, source):
@@ -71,7 +107,7 @@
     head_group = heads_q // heads_kv
     whole_rows, whole_query = (
         lax.all_gather(context_block_rows, "tp", axis=1, tiled=True),
-        lax.all_gather(query_hidden_rows, "tp", axis=1, tiled=True),
+        _save_loads(query_hidden_rows),
     )
     stacked = jnp.concatenate([whole_rows, whole_query], 0)
     head_rows = blk + qcount

time: 690 us -> 664 us (0.962)
  waiting for transfers between devices: 440 us -> 409 us
    all_gather x1 -> x0, waiting for transfers between devices: 19.5 us -> none  [on_device(): lax.all_gather(query_hidden_rows, 'tp', axis=1, tiled=True)]
    all_gather x1, waiting for transfers between devices: 47.3 us -> 32.6 us  [on_device(): lax.all_gather(context_block_rows, 'tp', axis=1, tiled=True)]
    ppermute x0 -> x7, waiting for transfers between devices: none -> 9.7 us  [the longest x4 9.69 us: measure_the_weights(): opened = lax.ppermute(a_now[-1] if a_now else array_in, chip_axis, panels)]
  transfers between devices with their start and end apart: 7 -> 13, of which waited for: 7 -> 9; matrix products, arithmetic and copies ran while one was open for 13% -> 13% of each run, Pallas kernels for 0% -> 0%
where the time goes in v1:
time: 664 us
  waiting for transfers between devices  409 us (62%)
  blocking collectives  144 us (22%)
  matrix products  51.5 us (8%)
  other arithmetic  23.5 us (4%)
  local copies, waits for them, and re-layouts  16.3 us (2%)
  between operations  14.5 us (2%)
    all_gather x1, waiting for transfers between devices, on_device(): lax.all_gather(query_matrix, 'ctx', axis=0, tiled=True)  133 us
    all_gather x1, waiting for transfers between devices, on_device(): lax.all_gather(key_matrix, 'ctx', axis=0, tiled=True)  73.3 us
    psum x1, blocking collectives, on_device(): lax.psum((total * scaled, mixed * scaled[..., None]), 'ctx')  72.5 us
    pmax x1, blocking collectives, on_device(): top = lax.pmax(peak, 'ctx')  71.4 us
    all_gather x1, waiting for transfers between devices, on_device(): lax.all_gather(value_matrix, 'ctx', axis=0, tiled=True)  69.1 us
    psum x1, waiting for transfers between devices, from_root(): return lax.psum(kept, axis)  47.8 us
    psum x1, waiting for transfers between devices, on_device(): lax.psum((total * scaled, mixed * scaled[..., None]), 'ctx')  41.1 us
    all_gather x1, waiting for transfers between devices, on_device(): lax.all_gather(context_block_rows, 'tp', axis=1, tiled=True)  32.6 us
  transfers between devices with their start and end apart: 13, of which 9 were waited for; matrix products, arithmetic and copies ran while one was open for 13% of the time, Pallas kernels for 0%

profile of v1, /device:TPU:2, one launch (start us, length us, event | category | flops | bytes accessed | tf_op | source)
XLA Modules:
  0.0 663.9 jit_solution(9031458284458859280)
XLA Ops:
  7.2 0.0 all-gather.5.cloned.1.call-start
  7.2 0.7 all-gather.5.cloned.1.call-update
  7.9 0.0 all-gather.9.cloned.1.call-start
  7.9 0.7 all-gather.9.cloned.1.call-update
  8.6 0.0 all-gather.7.cloned.1.call-start
  8.7 0.7 all-gather.7.cloned.1.call-update
  9.4 0.0 all-gather.11.cloned.1.call-start
  9.4 0.5 all-gather.11.cloned.1.call-update
  10.0 0.0 all-reduce.7.cloned.1.call-start
  10.0 0.0 collective-permute-start
  10.0 1.7 collective-permute-start.4
  11.8 0.7 convert_element_type.69
  12.4 2.5 multiply_cosine_fusion
  14.9 0.8 multiply_cosine_fusion.3
  15.8 0.0 collective-permute-start.1
  15.8 1.4 broadcast_compare_fusion
  17.2 3.0 collective-permute-done.1
  20.2 0.1 iota_compare_fusion
  20.3 1.8 collective-permute-start.5
  22.0 2.5 collective-permute-done.2
  24.6 0.9 concatenate.62
  25.5 1.7 collective-permute-start.6
  27.2 4.1 collective-permute-done.3
  31.4 0.9 bitcast_dynamic-update-slice_fusion.3
  32.4 0.6 gather_fusion
  33.0 0.1 copy.39
  33.1 32.6 %all-gather.5.cloned.1.call-done = bf16[512,8192]{1,0:T(8,128)(2,1)} async-done(((bf16[512,1024]{1,0:T(8,128)(2,1)}), bf16[512,8192]{1,0:T(8,128)(2,1)}) %all-gather.5.cloned.1.call-update) | async-done | bytes 8388624 | tf_op jit(solution)/shard_map/all_gather | solution.py:109
  65.7 7.6 %constant_dynamic-update-slice_fusion.1 = bf16[576,8192]{1,0:T(8,128)(2,1)} fusion(bf16[512,8192]{1,0:T(8,128)(2,1)} %all-gather.5.cloned.1.call-done), kind=kLoop, calls=%fused_computation.103 | loop fusion | bytes 16777216
  73.3 1.1 constant_dynamic-update-slice_fusion
  74.4 73.3 %all-gather.9.cloned.1.call-done = bf16[8192,128]{1,0:T(8,128)(2,1)} async-done(((bf16[256,128]{1,0:T(8,128)(2,1)}), bf16[8192,128]{1,0:T(8,128)(2,1)}) %all-gather.9.cloned.1.call-update) | async-done | bytes 2097168 | tf_op jit(solution)/shard_map/all_gather | solution.py:121
  147.7 5.8 fusion.85
  153.6 1.2 fusion.35
  154.8 0.8 maximum_select_fusion
  155.6 0.8 fusion.64
  156.4 69.1 %all-gather.7.cloned.1.call-done = bf16[8192,128]{1,0:T(8,128)(2,1)} async-done(((bf16[256,128]{1,0:T(8,128)(2,1)}), bf16[8192,128]{1,0:T(8,128)(2,1)}) %all-gather.7.cloned.1.call-update) | async-done | bytes 2097168 | tf_op jit(solution)/shard_map/all_gather | solution.py:126
  225.5 6.9 %convolution_convert_fusion = bf16[576,128]{1,0:T(8,128)(2,1)S(1)} fusion(bf16[576,8192]{1,0:T(8,128)(2,1)} %constant_dynamic-update-slice_fusion, bf16[8192,128]{1,0:T(8,128)(2,1)} %all-gather.7.cloned.1.call-done), kind=kOutput, calls=%fused_computation.27 | convolution fusion | flops 1208033280 | bytes 11681792 | tf_op jit(solution)/shard_map/dot_general | solution.py:124
  232.4 0.8 slice_bitcast_fusion.3
  233.2 0.0 all-reduce.5.cloned.1.call-start
  233.2 132.5 %all-gather.11.cloned.1.call-done = bf16[8192,1024]{1,0:T(8,128)(2,1)} async-done(((bf16[256,1024]{1,0:T(8,128)(2,1)}), bf16[8192,1024]{1,0:T(8,128)(2,1)}) %all-gather.11.cloned.1.call-update) | async-done | bytes 16777232 | tf_op jit(solution)/shard_map/all_gather | solution.py:116
  365.8 14.9 %fusion.86 = f32[576,1024]{1,0:T(8,128)S(1)} fusion(bf16[576,8192]{1,0:T(8,128)(2,1)} %constant_dynamic-update-slice_fusion, bf16[8192,1024]{1,0:T(8,128)(2,1)} %all-gather.11.cloned.1.call-done), kind=kOutput, calls=%fused_computation.142 | convolution fusion | flops 9663676416 | bytes 28573696 | tf_op jit(solution)/shard_map/dot_general | solution.py:114
  380.7 0.1 slice_bitcast_fusion
  380.9 0.1 fusion.82
  381.1 0.1 subtract_convert_fusion.1
  381.2 1.4 fusion.83
  382.6 1.0 fusion.25
  383.5 71.4 %pmax.7 = f32[64,1,8]{0,2,1:T(8,128)S(1)} all-reduce(f32[64,1,8]{0,2,1:T(8,128)S(1)} %bitcast.192), channel_id=1, replica_groups=mesh['ctx'=32,'tp'=8] {'ctx'}, use_global_device_ids=true, to_apply=%region_5.6 | all-reduce | flops 512 | bytes 4096 | tf_op jit(solution)/shard_map/pmax | solution.py:168
  455.0 0.5 copy.40
  455.5 2.0 fusion.81
  457.5 0.6 bitcast_multiply_fusion.1
  458.1 1.1 fusion.14
  459.1 0.0 all-reduce.5.cloned.1.call-update
  459.1 3.5 subtract_convert_fusion
  462.6 47.8 %all-reduce.7.cloned.1.call-done = (bf16[512,1,128]{2,0,1:T(8,128)(2,1)}, bf16[512,1,128]{2,0,1:T(8,128)(2,1)}) async-done(((bf16[512,1,128]{2,0,1:T(8,128)(2,1)}, bf16[512,1,128]{2,0,1:T(8,128)(2,1)}), (bf16[512,1,128]{2,0,1:T(8,128)(2,1)}, bf16[512,1,128]{2,0,1:T(8,128)(2,1)})) %all-reduce.7.cloned.1.call-update) | async-done | bytes 262160 | tf_op jit(solution)/shard_map/psum | solution.py:48
  510.4 10.7 %fusion.2 = (f32[512,8]{0,1:T(8,128)S(1)}, f32[1024,512,8]{1,0,2:T(8,128)}) fusion(pred[512,1024]{0,1:T(8,128)(4,1)} %concatenate.62, bf16[512,8,64]{2,0,1:T(8,128)(2,1)} %get-tuple-element.9, bf16[512,8,64]{2,0,1:T(8,128)(2,1)S(1)} %get-tuple-element.8, bf16[512,1,64]{2,0,1:T(8,128)(2,1)} %copy-done.1, bf16[512,1,64]{2,0,1:T(8,128)(2,1)S(1)} %get-tuple-element.14, ...), kind=kOutput, calls=%fused_computation.5 | convolution fusion | flops 1089204224 | bytes 18628608 | tf_op jit(solution)/shard_map/qkgd,skd->qkgs/dot_general | solution.py:80
  521.2 9.3 %fusion = f32[512,8]{0,1:T(8,128)S(1)} fusion(f32[1024,512,8]{1,0,2:T(8,128)} %get-tuple-element.32, f32[512,8]{0,1:T(8,128)S(1)} %get-tuple-element.31, pred[512,1024]{0,1:T(8,128)(4,1)S(1)} %copy-done), kind=kLoop, calls=%fused_computation.3 | loop fusion | flops 16773120 | bytes 17334272 | tf_op jit(solution)/shard_map/reduce_sum | solution.py:86
  530.4 0.3 fusion.84
  530.8 9.1 %fusion.7 = bf16[1,128,512,8]{2,1,3,0:T(8,128)(2,1)S(1)} fusion(f32[1024,512,8]{1,0,2:T(8,128)} %get-tuple-element.32, f32[512,8]{0,1:T(8,128)S(1)} %get-tuple-element.31, pred[512,1024]{0,1:T(8,128)(4,1)S(1)} %copy-done, f32[512,8]{0,1:T(8,128)S(1)} %fusion, bf16[512,1,128]{2,0,1:T(8,128)(2,1)S(1)} %copy-done.4, bf16[512,1,128]{2,0,1:T(8,128)(2,1)S(1)} %copy-done.10), kind=kOutput, calls=%fused_computation.11 | convolution fusion | flops 1092091904 | bytes 18644992 | tf_op jit(solution)/shard_map/qkgs,skd->qkgd/dot_general | solution.py:87
  539.9 0.1 fusion.44
  540.0 1.3 copy.30
  541.3 72.5 %psum.31 = f32[64,1,8]{0,2,1:T(8,128)S(1)} all-reduce(f32[64,1,8]{0,2,1:T(8,128)S(1)} %copy-done.8), channel_id=1, replica_groups=mesh['ctx'=32,'tp'=8] {'ctx'}, use_global_device_ids=true, to_apply=%region_9.10 | all-reduce | flops 512 | bytes 4096 | tf_op jit(solution)/shard_map/psum | solution.py:170
  613.9 41.1 %all-reduce.5.cloned.1.call-done = f32[64,1,8,128]{3,0,2,1:T(8,128)} async-done(((f32[64,1,8,128]{3,0,2,1:T(8,128)}), f32[64,1,8,128]{3,0,2,1:T(8,128)}) %all-reduce.5.cloned.1.call-update) | async-done | bytes 262160 | tf_op jit(solution)/shard_map/psum | solution.py:170
  655.0 1.3 fusion.19
  656.3 0.1 copy.29
  656.4 0.7 copy.52
  (46 shorter events, 0.3 us)
Async XLA Ops:
  7.2 58.5 %all-gather.5.cloned.1.call-start = ((), (), s32[]{:S(2)}) async-start(), calls=%async_computation | async-start | bytes 9437184 | tf_op jit(solution)/shard_map/all_gather | solution.py:109
  7.9 139.8 %all-gather.9.cloned.1.call-start = ((), (), s32[]{:S(2)}) async-start(), calls=%async_computation.2 | async-start | bytes 2162688 | tf_op jit(solution)/shard_map/all_gather | solution.py:121
  8.6 216.8 %all-gather.7.cloned.1.call-start = ((), (), s32[]{:S(2)}) async-start(), calls=%async_computation.1 | async-start | bytes 2162688 | tf_op jit(solution)/shard_map/all_gather | solution.py:126
  9.4 356.4 %all-gather.11.cloned.1.call-start = ((), (), s32[]{:S(2)}) async-start(), calls=%async_computation.3 | async-start | bytes 17301504 | tf_op jit(solution)/shard_map/all_gather | solution.py:116
  10.0 500.5 %all-reduce.7.cloned.1.call-start = ((), (), s32[]{:S(2)}) async-start(), calls=%async_computation.5 | async-start | bytes 524288 | tf_op jit(solution)/shard_map/psum | solution.py:48
  10.0 5.8 collective-permute-start
  10.0 10.2 %collective-permute-start.4 = (bf16[64,1024]{1,0:T(8,128)(2,1)}, bf16[64,1024]{1,0:T(8,128)(2,1)S(1)}, u32[]{:S(2)}, u32[]{:S(2)}) collective-permute-start(bf16[64,1024]{1,0:T(8,128)(2,1)} %param.12), channel_id=1, source_target_pairs={{1,0},{2,1},{3,2},{4,3},{5,4},{6,5},{7,6},{0,7},{9,8},{10,9},{11,1... | collective-permute-start | bytes 393224 | tf_op jit(solution)/shard_map/ppermute | solution.py:34
  15.8 4.4 collective-permute-start.1
  20.2 4.4 collective-permute-start.2
  20.3 5.2 collective-permute-start.5
  24.6 6.8 %collective-permute-start.3 = (bf16[64,1024]{1,0:T(8,128)(2,1)S(1)}, bf16[64,1024]{1,0:T(8,128)(2,1)S(1)}, u32[]{:S(2)}, u32[]{:S(2)}) collective-permute-start(bf16[64,1024]{1,0:T(8,128)(2,1)S(1)} %collective-permute-done.2), channel_id=1, source_target_pairs={{0,1},{1,2},{2,3},{3,4},{4,5},{5,6},{6,7},{7,0},{8,9},{9,10},{10,1... | collective-permute-start | bytes 393224 | tf_op jit(solution)/shard_map/ppermute | solution.py:31
  25.5 6.9 %collective-permute-start.6 = (bf16[64,1024]{1,0:T(8,128)(2,1)S(1)}, bf16[64,1024]{1,0:T(8,128)(2,1)S(1)}, u32[]{:S(2)}, u32[]{:S(2)}) collective-permute-start(bf16[64,1024]{1,0:T(8,128)(2,1)S(1)} %collective-permute-done.5), channel_id=1, source_target_pairs={{1,0},{2,1},{3,2},{4,3},{5,4},{6,5},{7,6},{0,7},{9,8},{10,9},{11,1... | collective-permute-start | bytes 393224 | tf_op jit(solution)/shard_map/ppermute | solution.py:34
  73.3 80.3 %copy-start.9 = (f32[64]{0:T(128)S(1)}, f32[64]{0:T(128)}, u32[]{:S(2)}) copy-start(f32[64]{0:T(128)} %constant.46.clone) | copy-start | bytes 772
  154.8 225.9 %copy-start.1 = (bf16[512,1,64]{2,0,1:T(8,128)(2,1)}, bf16[512,1,64]{2,0,1:T(8,128)(2,1)S(1)}, u32[]{:S(2)}) copy-start(bf16[512,1,64]{2,0,1:T(8,128)(2,1)S(1)} %get-tuple-element.15) | copy-start | bytes 196612
  232.4 133.4 %copy-start.2 = (bf16[576,128]{1,0:T(8,128)(2,1)}, bf16[576,128]{1,0:T(8,128)(2,1)S(1)}, u32[]{:S(2)}) copy-start(bf16[576,128]{1,0:T(8,128)(2,1)S(1)} %convolution_convert_fusion) | copy-start | bytes 442372
  233.2 421.8 %all-reduce.5.cloned.1.call-start = ((), (), s32[]{:S(2)}) async-start(), calls=%async_computation.4 | async-start | bytes 524288 | tf_op jit(solution)/shard_map/psum | solution.py:170
  455.0 2.5 copy-start.7
  455.0 3.1 copy-start.3
  510.4 10.7 %copy-start = (pred[512,1024]{0,1:T(8,128)(4,1)S(1)}, pred[512,1024]{0,1:T(8,128)(4,1)}, u32[]{:S(2)}) copy-start(pred[512,1024]{0,1:T(8,128)(4,1)} %concatenate.62) | copy-start | bytes 1572868
  521.1 9.3 %copy-start.5 = (bf16[64,64]{1,0:T(8,128)(2,1)S(1)}, bf16[64,64]{1,0:T(8,128)(2,1)}, u32[]{:S(2)}) copy-start(bf16[64,64]{1,0:T(8,128)(2,1)} %get-tuple-element.20) | copy-start | bytes 24580
  521.1 9.3 %copy-start.6 = (bf16[64,64]{1,0:T(8,128)(2,1)S(1)}, bf16[64,64]{1,0:T(8,128)(2,1)}, u32[]{:S(2)}) copy-start(bf16[64,64]{1,0:T(8,128)(2,1)} %get-tuple-element.21) | copy-start | bytes 24580
  521.1 9.6 %copy-start.4 = (bf16[512,1,128]{2,0,1:T(8,128)(2,1)S(1)}, bf16[512,1,128]{2,0,1:T(8,128)(2,1)}, u32[]{:S(2)}) copy-start(bf16[512,1,128]{2,0,1:T(8,128)(2,1)} %get-tuple-element.18) | copy-start | bytes 393220
  521.1 9.6 %copy-start.10 = (bf16[512,1,128]{2,0,1:T(8,128)(2,1)S(1)}, bf16[512,1,128]{2,0,1:T(8,128)(2,1)}, u32[]{:S(2)}) copy-start(bf16[512,1,128]{2,0,1:T(8,128)(2,1)} %get-tuple-element.7) | copy-start | bytes 393220
  530.8 10.5 %copy-start.8 = (f32[64,1,8]{0,2,1:T(8,128)S(1)}, f32[64,1,8]{0,2,1:T(8,128)}, u32[]{:S(2)}) copy-start(f32[64,1,8]{0,2,1:T(8,128)} %get-tuple-element.25) | copy-start | bytes 6148
Sparse Core Ops, SparseCore 0:
  9.8 55.8 all-gather.4
  68.3 79.3 all-gather.8
  150.3 75.1 all-gather.6
  227.9 137.7 all-gather.10
  369.1 141.2 all-reduce.6
  513.8 141.1 all-reduce.4
